TPU v7x, 256 devices: a whole 4x4x8 slice. The times are simulated.
256 devices in a mesh: outer: 16 (over x, y), inner: 16 (over z, core).
Axes of the slice: x: 4, y: 4, z: 8, core: 2. Of those that a mesh axis runs over, the one named last changes fastest.
Arguments:
- queries: bfloat16 [65536, 1024], P(('outer', 'inner')), may hold values from -6 to 6
- out_grad: bfloat16 [65536, 1024], P(('outer', 'inner')), may hold values from -1.5 to 1.5
- logsumexp: float32 [8, 65536], P(None, ('outer', 'inner')), may hold values from 4 to 8
- row_delta: float32 [8, 65536], P(None, ('outer', 'inner')), may hold values from -6 to 6
- doc_offset: int32 [65536], P(('outer', 'inner')), may hold values from 0 to 3071, as said below
- key_states: bfloat16 [65536, 128], P(('outer', 'inner')), may hold values from -6 to 6
- value_states: bfloat16 [65536, 128], P(('outer', 'inner')), may hold values from -6 to 6
Outputs:
- query_grad: bfloat16 [65536, 1024], P(('outer', 'inner'))
- key_grad: bfloat16 [65536, 128], P(('outer', 'inner'))
- value_grad: bfloat16 [65536, 128], P(('outer', 'inner'))
Inputs may be any that keep to these rules, and one draw needn't show every extreme that they name: `doc_offset`: documents are contiguous runs of tokens whose entries count 0, 1, 2, ...; a new document starts wherever the entry is 0. Each document holds at most 3072 tokens and one holds exactly 3072.
All inputs are finite; a program needn't handle non-finite values.
Results may differ from a plain program's by a relative error of at most 0.0054.
Values may be sent and summed in bfloat16 or wider, within the bound.
A program may use at most 128 MiB of HBM per device.

v0:
```python
import math

import jax
import jax.numpy as jnp
from jax import lax
from jax.sharding import PartitionSpec as P

REACH = 12


def shifted(block, axis, distance):
    devices = range(lax.axis_size(axis))
    route = [(i - distance, i) for i in devices if i - distance in devices]
    return lax.ppermute(block, axis, route)


def pair_grads(
    queries, out_grad, logsumexp, row_delta, row_first, query_pos, key_states, value_states, key_pos
):
    head_size = key_states.shape[1]
    head_count = logsumexp.shape[0]
    inv_root = 1.0 / math.sqrt(head_size)
    allowed = (key_pos[None, :] <= query_pos[:, None]) & (key_pos[None, :] >= row_first[:, None])
    zero_keys = jnp.zeros(key_states.shape, jnp.float32)
    zero_rows = jnp.zeros(queries.shape, jnp.float32)

    def one_head(running, head_idx):
        grad_q, grad_k, grad_v = running
        query_h = lax.dynamic_slice_in_dim(queries, head_idx * head_size, head_size, 1)
        dout_h = lax.dynamic_slice_in_dim(out_grad, head_idx * head_size, head_size, 1)
        norm_h = lax.dynamic_index_in_dim(logsumexp, head_idx, 0, keepdims=False)
        delta_h = lax.dynamic_index_in_dim(row_delta, head_idx, 0, keepdims=False)
        scores = jnp.dot(query_h, key_states.T, preferred_element_type=jnp.float32) * inv_root
        prob = jnp.where(allowed, jnp.exp(scores - norm_h[:, None]), jnp.zeros_like(scores))
        prob_b = prob.astype(jnp.bfloat16)
        dprob = jnp.dot(dout_h, value_states.T, preferred_element_type=jnp.float32)
        dscore = (prob * (dprob - delta_h[:, None])).astype(jnp.bfloat16)
        piece = jnp.dot(dscore, key_states, preferred_element_type=jnp.float32) * inv_root
        grad_q = lax.dynamic_update_slice_in_dim(grad_q, piece, head_idx * head_size, 1)
        grad_k = grad_k + jnp.dot(dscore.T, query_h, preferred_element_type=jnp.float32) * inv_root
        grad_v = grad_v + jnp.dot(prob_b.T, dout_h, preferred_element_type=jnp.float32)
        return ((grad_q, grad_k, grad_v), None)

    results, _ = lax.scan(
        one_head, (zero_rows, zero_keys, zero_keys), jnp.arange(head_count, dtype=jnp.int32)
    )
    return results


def guarded_grads(
    queries, out_grad, logsumexp, row_delta, row_first, query_pos, key_states, value_states, key_pos
):
    return pair_grads(
        queries,
        out_grad,
        logsumexp,
        row_delta,
        row_first,
        query_pos,
        key_states,
        value_states,
        key_pos,
    )


def on_device(queries, out_grad, logsumexp, row_delta, doc_offset, key_states, value_states):
    local_rows = queries.shape[0]
    my_index = lax.axis_index(("outer", "inner"))
    query_pos = my_index * local_rows + jnp.arange(local_rows, dtype=jnp.int32)
    query_first = query_pos - doc_offset
    grad_q, grad_k, grad_v = pair_grads(
        queries,
        out_grad,
        logsumexp,
        row_delta,
        query_first,
        query_pos,
        key_states,
        value_states,
        query_pos,
    )
    for distance in range(1, REACH + 1):
        near_key, near_value = shifted((key_states, value_states), ("outer", "inner"), distance)
        near_pos = query_pos - distance * local_rows
        part_q, part_k, part_v = guarded_grads(
            queries,
            out_grad,
            logsumexp,
            row_delta,
            query_first,
            query_pos,
            near_key,
            near_value,
            near_pos,
        )
        grad_q = grad_q + part_q
        back_k, back_v = shifted((part_k, part_v), ("outer", "inner"), -distance)
        grad_k = grad_k + back_k
        grad_v = grad_v + back_v
    return (grad_q.astype(jnp.bfloat16), grad_k.astype(jnp.bfloat16), grad_v.astype(jnp.bfloat16))


def solution(mesh):
    return jax.shard_map(
        on_device,
        mesh=mesh,
        in_specs=(
            P(("outer", "inner"), None),
            P(("outer", "inner"), None),
            P(None, ("outer", "inner")),
            P(None, ("outer", "inner")),
            P(("outer", "inner")),
            P(("outer", "inner"), None),
            P(("outer", "inner"), None),
        ),
        out_specs=(
            P(("outer", "inner"), None),
            P(("outer", "inner"), None),
            P(("outer", "inner"), None),
        ),
        check_vma=False,
    )
```

profile of v0, /device:TPU:37, one launch (start us, length us, event | category | flops | bytes accessed | tf_op | source)
XLA Modules:
  0.0 1277.7 jit_solution(17514450841220054852)
XLA Ops:
  10.5 4.8 collective-permute-start.3
  32.7 83.3 %while.196 = (s32[]{:T(128)}, f32[256,1024]{1,0:T(8,128)S(1)}, f32[256,128]{1,0:T(8,128)}, f32[256,128]{1,0:T(8,128)}, s32[8]{0:T(128)S(1)}, /*index=5*/bf16[256...) while((s32[]{:T(128)}, f32[256,1024]{1,0:T(8,128)S(1)}, ...), condition=%wide.region_3.4_spmd.clone, body=%wide.region_2.3_spmd.clone.sunk | while | flops 84738056 | bytes 3364648 | solution.py:44
  120.4 6.6 collective-permute-start.8
  128.1 80.8 %while.197 = (s32[]{:T(128)}, f32[256,1024]{1,0:T(8,128)}, f32[256,128]{1,0:T(8,128)S(1)}, f32[256,128]{1,0:T(8,128)}, s32[8]{0:T(128)S(1)}, /*index=5*/bf16[256...) while((s32[]{:T(128)}, f32[256,1024]{1,0:T(8,128)}, ...), condition=%wide.region_5.6_spmd.clone, body=%wide.region_4.5_spmd.clone.sunk | while | flops 84738056 | bytes 3364592 | solution.py:44
  215.1 92.4 %while.198 = (s32[]{:T(128)}, f32[256,1024]{1,0:T(8,128)S(1)}, f32[256,128]{1,0:T(8,128)}, f32[256,128]{1,0:T(8,128)}, s32[8]{0:T(128)S(1)}, /*index=5*/bf16[256...) while((s32[]{:T(128)}, f32[256,1024]{1,0:T(8,128)S(1)}, ...), condition=%wide.region_7.8_spmd.clone, body=%wide.region_6.7_spmd.clone.sunk | while | flops 84738056 | bytes 2315960 | solution.py:44
  307.5 5.7 collective-permute-start.11
  318.7 80.9 %while.199 = (s32[]{:T(128)}, f32[256,1024]{1,0:T(8,128)}, f32[256,128]{1,0:T(8,128)S(1)}, f32[256,128]{1,0:T(8,128)}, s32[8]{0:T(128)S(1)}, /*index=5*/bf16[256...) while((s32[]{:T(128)}, f32[256,1024]{1,0:T(8,128)}, ...), condition=%wide.region_9.10_spmd.clone, body=%wide.region_8.9_spmd.clone.sunk | while | flops 84738056 | bytes 3364592 | solution.py:44
  399.6 5.3 collective-permute-start.13
  408.7 92.4 %while.200 = (s32[]{:T(128)}, f32[256,1024]{1,0:T(8,128)S(1)}, f32[256,128]{1,0:T(8,128)}, f32[256,128]{1,0:T(8,128)}, s32[8]{0:T(128)S(1)}, /*index=5*/bf16[256...) while((s32[]{:T(128)}, f32[256,1024]{1,0:T(8,128)S(1)}, ...), condition=%wide.region_11.12_spmd.clone, body=%wide.region_10.11_spmd.clone.sunk | while | flops 84738056 | bytes 2315960 | solution.py:44
  501.1 5.9 collective-permute-start.15
  507.0 4.8 collective-permute-start.16
  512.9 80.7 %while.201 = (s32[]{:T(128)}, f32[256,1024]{1,0:T(8,128)}, f32[256,128]{1,0:T(8,128)S(1)}, f32[256,128]{1,0:T(8,128)}, s32[8]{0:T(128)S(1)}, /*index=5*/bf16[256...) while((s32[]{:T(128)}, f32[256,1024]{1,0:T(8,128)}, ...), condition=%wide.region_13.14_spmd.clone, body=%wide.region_12.13_spmd.clone.sunk | while | flops 84738056 | bytes 3364592 | solution.py:44
  593.6 5.3 collective-permute-start.17
  603.2 75.9 %while.202 = (s32[]{:T(128)}, f32[256,1024]{1,0:T(8,128)S(1)}, f32[256,128]{1,0:T(8,128)S(1)}, f32[256,128]{1,0:T(8,128)}, s32[8]{0:T(128)S(1)}, /*index=5*/bf16...) while((s32[]{:T(128)}, f32[256,1024]{1,0:T(8,128)S(1)}, ...), condition=%wide.region_15.16_spmd.clone, body=%wide.region_14.15_spmd.clone.sunk | while | flops 84738056 | bytes 2307720 | solution.py:44
  683.3 7.9 collective-permute-start.20
  692.3 75.3 %while.203 = (s32[]{:T(128)}, f32[256,1024]{1,0:T(8,128)}, f32[256,128]{1,0:T(8,128)S(1)}, f32[256,128]{1,0:T(8,128)}, s32[8]{0:T(128)S(1)}, /*index=5*/bf16[256...) while((s32[]{:T(128)}, f32[256,1024]{1,0:T(8,128)}, ...), condition=%wide.region_17.18_spmd.clone, body=%wide.region_16.17_spmd.clone.sunk | while | flops 84738056 | bytes 3356352 | solution.py:44
  772.2 75.9 %while.204 = (s32[]{:T(128)}, f32[256,1024]{1,0:T(8,128)S(1)}, f32[256,128]{1,0:T(8,128)S(1)}, f32[256,128]{1,0:T(8,128)}, s32[8]{0:T(128)S(1)}, /*index=5*/bf16...) while((s32[]{:T(128)}, f32[256,1024]{1,0:T(8,128)S(1)}, ...), condition=%wide.region_19.20_spmd.clone, body=%wide.region_18.19_spmd.clone.sunk | while | flops 84738056 | bytes 2307720 | solution.py:44
  853.5 75.3 %while.205 = (s32[]{:T(128)}, f32[256,1024]{1,0:T(8,128)}, f32[256,128]{1,0:T(8,128)S(1)}, f32[256,128]{1,0:T(8,128)}, s32[8]{0:T(128)S(1)}, /*index=5*/bf16[256...) while((s32[]{:T(128)}, f32[256,1024]{1,0:T(8,128)}, ...), condition=%wide.region_21.22_spmd.clone, body=%wide.region_20.21_spmd.clone.sunk | while | flops 84738056 | bytes 3356352 | solution.py:44
  931.4 6.3 collective-permute-start.38
  937.8 5.7 collective-permute-start.39
  944.2 75.9 %while.206 = (s32[]{:T(128)}, f32[256,1024]{1,0:T(8,128)S(1)}, f32[256,128]{1,0:T(8,128)S(1)}, f32[256,128]{1,0:T(8,128)}, s32[8]{0:T(128)S(1)}, /*index=5*/bf16...) while((s32[]{:T(128)}, f32[256,1024]{1,0:T(8,128)S(1)}, ...), condition=%wide.region_23.24_spmd.clone, body=%wide.region_22.23_spmd.clone.sunk | while | flops 84738056 | bytes 2307720 | solution.py:44
  1023.7 7.1 collective-permute-start.41
  1034.6 6.6 collective-permute-start.43
  1046.7 75.5 %while.207 = (s32[]{:T(128)}, f32[256,1024]{1,0:T(8,128)}, f32[256,128]{1,0:T(8,128)S(1)}, f32[256,128]{1,0:T(8,128)}, s32[8]{0:T(128)S(1)}, /*index=5*/bf16[256...) while((s32[]{:T(128)}, f32[256,1024]{1,0:T(8,128)}, ...), condition=%wide.region_25.26_spmd.clone, body=%wide.region_24.25_spmd.clone.sunk | while | flops 84738056 | bytes 3356352 | solution.py:44
  1122.2 6.6 collective-permute-start.45
  1130.7 4.9 collective-permute-start.47
  1141.9 64.7 %while.195 = (s32[]{:T(128)}, f32[256,1024]{1,0:T(8,128)S(1)}, f32[256,128]{1,0:T(8,128)S(1)}, f32[256,128]{1,0:T(8,128)S(1)}, s32[8]{0:T(128)S(1)}, /*index=5*/...) while((s32[]{:T(128)}, f32[256,1024]{1,0:T(8,128)S(1)}, ...), condition=%wide.region_1.2_spmd.clone, body=%wide.region_0.1_spmd.clone.sunk | while | flops 84738056 | bytes 2311844 | solution.py:44
  1217.0 6.1 collective-permute-start.29
  1227.0 6.7 add_convert_fusion
  1233.7 5.4 collective-permute-start.31
  1256.0 6.3 collective-permute-done.33
  1262.3 11.1 collective-permute-done.34
  (2011 shorter events, 883.4 us)
Async XLA Ops:
  4.7 111.3 %collective-permute-start.2 = (bf16[256,128]{1,0:T(8,128)(2,1)}, bf16[256,128]{1,0:T(8,128)(2,1)}, u32[]{:S(2)}, u32[]{:S(2)}) collective-permute-start(bf16[256,128]{1,0:T(8,128)(2,1)} %param.38), channel_id=1, source_target_pairs={{0,2},{1,3},{2,4},{3,5},{4,6},{5,7},{6,8},{7,9},{8,10},{9,11},{10,... | collective-permute-start | bytes 196616 | tf_op jit(solution)/shard_map/ppermute | solution.py:14
  10.5 109.8 %collective-permute-start.3 = (bf16[256,128]{1,0:T(8,128)(2,1)}, bf16[256,128]{1,0:T(8,128)(2,1)}, u32[]{:S(2)}, u32[]{:S(2)}) collective-permute-start(bf16[256,128]{1,0:T(8,128)(2,1)} %param.39), channel_id=1, source_target_pairs={{0,2},{1,3},{2,4},{3,5},{4,6},{5,7},{6,8},{7,9},{8,10},{9,11},{10,... | collective-permute-start | bytes 196616 | tf_op jit(solution)/shard_map/ppermute | solution.py:14
  15.3 193.6 %collective-permute-start.4 = (bf16[256,128]{1,0:T(8,128)(2,1)}, bf16[256,128]{1,0:T(8,128)(2,1)}, u32[]{:S(2)}, u32[]{:S(2)}) collective-permute-start(bf16[256,128]{1,0:T(8,128)(2,1)} %param.38), channel_id=1, source_target_pairs={{0,3},{1,4},{2,5},{3,6},{4,7},{5,8},{6,9},{7,10},{8,11},{9,12},{10... | collective-permute-start | bytes 196616 | tf_op jit(solution)/shard_map/ppermute | solution.py:14
  27.0 183.8 %collective-permute-start.5 = (bf16[256,128]{1,0:T(8,128)(2,1)}, bf16[256,128]{1,0:T(8,128)(2,1)}, u32[]{:S(2)}, u32[]{:S(2)}) collective-permute-start(bf16[256,128]{1,0:T(8,128)(2,1)} %param.39), channel_id=1, source_target_pairs={{0,3},{1,4},{2,5},{3,6},{4,7},{5,8},{6,9},{7,10},{8,11},{9,12},{10... | collective-permute-start | bytes 196616 | tf_op jit(solution)/shard_map/ppermute | solution.py:14
  29.5 277.9 %collective-permute-start.6 = (bf16[256,128]{1,0:T(8,128)(2,1)}, bf16[256,128]{1,0:T(8,128)(2,1)}, u32[]{:S(2)}, u32[]{:S(2)}) collective-permute-start(bf16[256,128]{1,0:T(8,128)(2,1)} %param.38), channel_id=1, source_target_pairs={{0,4},{1,5},{2,6},{3,7},{4,8},{5,9},{6,10},{7,11},{8,12},{9,13},{1... | collective-permute-start | bytes 196616 | tf_op jit(solution)/shard_map/ppermute | solution.py:14
  116.0 197.1 %collective-permute-start.7 = (bf16[256,128]{1,0:T(8,128)(2,1)}, bf16[256,128]{1,0:T(8,128)(2,1)}, u32[]{:S(2)}, u32[]{:S(2)}) collective-permute-start(bf16[256,128]{1,0:T(8,128)(2,1)} %param.39), channel_id=1, source_target_pairs={{0,4},{1,5},{2,6},{3,7},{4,8},{5,9},{6,10},{7,11},{8,12},{9,13},{1... | collective-permute-start | bytes 196616 | tf_op jit(solution)/shard_map/ppermute | solution.py:14
  120.4 279.2 %collective-permute-start.8 = (bf16[256,128]{1,0:T(8,128)(2,1)}, bf16[256,128]{1,0:T(8,128)(2,1)}, u32[]{:S(2)}, u32[]{:S(2)}) collective-permute-start(bf16[256,128]{1,0:T(8,128)(2,1)} %param.38), channel_id=1, source_target_pairs={{0,5},{1,6},{2,7},{3,8},{4,9},{5,10},{6,11},{7,12},{8,13},{9,14},{... | collective-permute-start | bytes 196616 | tf_op jit(solution)/shard_map/ppermute | solution.py:14
  208.9 196.1 %collective-permute-start.9 = (bf16[256,128]{1,0:T(8,128)(2,1)}, bf16[256,128]{1,0:T(8,128)(2,1)}, u32[]{:S(2)}, u32[]{:S(2)}) collective-permute-start(bf16[256,128]{1,0:T(8,128)(2,1)} %param.39), channel_id=1, source_target_pairs={{0,5},{1,6},{2,7},{3,8},{4,9},{5,10},{6,11},{7,12},{8,13},{9,14},{... | collective-permute-start | bytes 196616 | tf_op jit(solution)/shard_map/ppermute | solution.py:14
  210.8 290.3 %collective-permute-start.10 = (bf16[256,128]{1,0:T(8,128)(2,1)}, bf16[256,128]{1,0:T(8,128)(2,1)}, u32[]{:S(2)}, u32[]{:S(2)}) collective-permute-start(bf16[256,128]{1,0:T(8,128)(2,1)} %param.38), channel_id=1, source_target_pairs={{0,6},{1,7},{2,8},{3,9},{4,10},{5,11},{6,12},{7,13},{8,14},{9,15},... | collective-permute-start | bytes 196616 | tf_op jit(solution)/shard_map/ppermute | solution.py:14
  307.5 199.5 %collective-permute-start.11 = (bf16[256,128]{1,0:T(8,128)(2,1)}, bf16[256,128]{1,0:T(8,128)(2,1)}, u32[]{:S(2)}, u32[]{:S(2)}) collective-permute-start(bf16[256,128]{1,0:T(8,128)(2,1)} %param.39), channel_id=1, source_target_pairs={{0,6},{1,7},{2,8},{3,9},{4,10},{5,11},{6,12},{7,13},{8,14},{9,15},... | collective-permute-start | bytes 196616 | tf_op jit(solution)/shard_map/ppermute | solution.py:14
  313.2 280.5 %collective-permute-start.12 = (bf16[256,128]{1,0:T(8,128)(2,1)}, bf16[256,128]{1,0:T(8,128)(2,1)}, u32[]{:S(2)}, u32[]{:S(2)}) collective-permute-start(bf16[256,128]{1,0:T(8,128)(2,1)} %param.38), channel_id=1, source_target_pairs={{0,7},{1,8},{2,9},{3,10},{4,11},{5,12},{6,13},{7,14},{8,15},{9,16}... | collective-permute-start | bytes 196616 | tf_op jit(solution)/shard_map/ppermute | solution.py:14
  399.6 199.3 %collective-permute-start.13 = (bf16[256,128]{1,0:T(8,128)(2,1)}, bf16[256,128]{1,0:T(8,128)(2,1)}, u32[]{:S(2)}, u32[]{:S(2)}) collective-permute-start(bf16[256,128]{1,0:T(8,128)(2,1)} %param.39), channel_id=1, source_target_pairs={{0,7},{1,8},{2,9},{3,10},{4,11},{5,12},{6,13},{7,14},{8,15},{9,16}... | collective-permute-start | bytes 196616 | tf_op jit(solution)/shard_map/ppermute | solution.py:14
  405.0 274.1 %collective-permute-start.14 = (bf16[256,128]{1,0:T(8,128)(2,1)}, bf16[256,128]{1,0:T(8,128)(2,1)}, u32[]{:S(2)}, u32[]{:S(2)}) collective-permute-start(bf16[256,128]{1,0:T(8,128)(2,1)} %param.38), channel_id=1, source_target_pairs={{0,8},{1,9},{2,10},{3,11},{4,12},{5,13},{6,14},{7,15},{8,16},{9,17... | collective-permute-start | bytes 196616 | tf_op jit(solution)/shard_map/ppermute | solution.py:14
  501.1 182.2 %collective-permute-start.15 = (bf16[256,128]{1,0:T(8,128)(2,1)}, bf16[256,128]{1,0:T(8,128)(2,1)}, u32[]{:S(2)}, u32[]{:S(2)}) collective-permute-start(bf16[256,128]{1,0:T(8,128)(2,1)} %param.39), channel_id=1, source_target_pairs={{0,8},{1,9},{2,10},{3,11},{4,12},{5,13},{6,14},{7,15},{8,16},{9,17... | collective-permute-start | bytes 196616 | tf_op jit(solution)/shard_map/ppermute | solution.py:14
  507.0 260.7 %collective-permute-start.16 = (bf16[256,128]{1,0:T(8,128)(2,1)}, bf16[256,128]{1,0:T(8,128)(2,1)}, u32[]{:S(2)}, u32[]{:S(2)}) collective-permute-start(bf16[256,128]{1,0:T(8,128)(2,1)} %param.38), channel_id=1, source_target_pairs={{0,9},{1,10},{2,11},{3,12},{4,13},{5,14},{6,15},{7,16},{8,17},{9,1... | collective-permute-start | bytes 196616 | tf_op jit(solution)/shard_map/ppermute | solution.py:14
  593.6 175.9 %collective-permute-start.17 = (bf16[256,128]{1,0:T(8,128)(2,1)}, bf16[256,128]{1,0:T(8,128)(2,1)}, u32[]{:S(2)}, u32[]{:S(2)}) collective-permute-start(bf16[256,128]{1,0:T(8,128)(2,1)} %param.39), channel_id=1, source_target_pairs={{0,9},{1,10},{2,11},{3,12},{4,13},{5,14},{6,15},{7,16},{8,17},{9,1... | collective-permute-start | bytes 196616 | tf_op jit(solution)/shard_map/ppermute | solution.py:14
  598.9 249.1 %collective-permute-start.18 = (bf16[256,128]{1,0:T(8,128)(2,1)}, bf16[256,128]{1,0:T(8,128)(2,1)}, u32[]{:S(2)}, u32[]{:S(2)}) collective-permute-start(bf16[256,128]{1,0:T(8,128)(2,1)} %param.38), channel_id=1, source_target_pairs={{0,10},{1,11},{2,12},{3,13},{4,14},{5,15},{6,16},{7,17},{8,18},{9,... | collective-permute-start | bytes 196616 | tf_op jit(solution)/shard_map/ppermute | solution.py:14
  679.1 170.9 %collective-permute-start.19 = (bf16[256,128]{1,0:T(8,128)(2,1)}, bf16[256,128]{1,0:T(8,128)(2,1)}, u32[]{:S(2)}, u32[]{:S(2)}) collective-permute-start(bf16[256,128]{1,0:T(8,128)(2,1)} %param.39), channel_id=1, source_target_pairs={{0,10},{1,11},{2,12},{3,13},{4,14},{5,15},{6,16},{7,17},{8,18},{9,... | collective-permute-start | bytes 196616 | tf_op jit(solution)/shard_map/ppermute | solution.py:14
  683.3 245.5 %collective-permute-start.20 = (bf16[256,128]{1,0:T(8,128)(2,1)}, bf16[256,128]{1,0:T(8,128)(2,1)}, u32[]{:S(2)}, u32[]{:S(2)}) collective-permute-start(bf16[256,128]{1,0:T(8,128)(2,1)} %param.38), channel_id=1, source_target_pairs={{0,11},{1,12},{2,13},{3,14},{4,15},{5,16},{6,17},{7,18},{8,19},{9,... | collective-permute-start | bytes 196616 | tf_op jit(solution)/shard_map/ppermute | solution.py:14
  767.6 163.8 %collective-permute-start.21 = (bf16[256,128]{1,0:T(8,128)(2,1)}, bf16[256,128]{1,0:T(8,128)(2,1)}, u32[]{:S(2)}, u32[]{:S(2)}) collective-permute-start(bf16[256,128]{1,0:T(8,128)(2,1)} %param.39), channel_id=1, source_target_pairs={{0,11},{1,12},{2,13},{3,14},{4,15},{5,16},{6,17},{7,18},{8,19},{9,... | collective-permute-start | bytes 196616 | tf_op jit(solution)/shard_map/ppermute | solution.py:14
  769.6 168.2 %collective-permute-start.22 = (bf16[256,128]{1,0:T(8,128)(2,1)}, bf16[256,128]{1,0:T(8,128)(2,1)}, u32[]{:S(2)}, u32[]{:S(2)}) collective-permute-start(bf16[256,128]{1,0:T(8,128)(2,1)} %param.38), channel_id=1, source_target_pairs={{0,12},{1,13},{2,14},{3,15},{4,16},{5,17},{6,18},{7,19},{8,20},{9,... | collective-permute-start | bytes 196616 | tf_op jit(solution)/shard_map/ppermute | solution.py:14
  848.0 172.0 %collective-permute-start.23 = (bf16[256,128]{1,0:T(8,128)(2,1)}, bf16[256,128]{1,0:T(8,128)(2,1)}, u32[]{:S(2)}, u32[]{:S(2)}) collective-permute-start(bf16[256,128]{1,0:T(8,128)(2,1)} %param.39), channel_id=1, source_target_pairs={{0,12},{1,13},{2,14},{3,15},{4,16},{5,17},{6,18},{7,19},{8,20},{9,... | collective-permute-start | bytes 196616 | tf_op jit(solution)/shard_map/ppermute | solution.py:14
  850.0 173.7 %collective-permute-start.36 = (f32[256,128]{1,0:T(8,128)}, f32[256,128]{1,0:T(8,128)}, u32[]{:S(2)}, u32[]{:S(2)}) collective-permute-start(f32[256,128]{1,0:T(8,128)} %get-tuple-element.862), channel_id=1, source_target_pairs={{1,0},{2,1},{3,2},{4,3},{5,4},{6,5},{7,6},{8,7},{9,8},{10,9},{11,1... | collective-permute-start | bytes 393224 | tf_op jit(solution)/shard_map/ppermute | solution.py:14
  928.8 102.0 %collective-permute-start.37 = (f32[256,128]{1,0:T(8,128)}, f32[256,128]{1,0:T(8,128)}, u32[]{:S(2)}, u32[]{:S(2)}) collective-permute-start(f32[256,128]{1,0:T(8,128)} %get-tuple-element.863), channel_id=1, source_target_pairs={{2,0},{3,1},{4,2},{5,3},{6,4},{7,5},{8,6},{9,7},{10,8},{11,9},{12,... | collective-permute-start | bytes 393224 | tf_op jit(solution)/shard_map/ppermute | solution.py:14
  931.4 103.1 %collective-permute-start.38 = (f32[256,128]{1,0:T(8,128)}, f32[256,128]{1,0:T(8,128)}, u32[]{:S(2)}, u32[]{:S(2)}) collective-permute-start(f32[256,128]{1,0:T(8,128)} %get-tuple-element.864), channel_id=1, source_target_pairs={{3,0},{4,1},{5,2},{6,3},{7,4},{8,5},{9,6},{10,7},{11,8},{12,9},{13... | collective-permute-start | bytes 393224 | tf_op jit(solution)/shard_map/ppermute | solution.py:14
  937.8 103.5 %collective-permute-start.39 = (f32[256,128]{1,0:T(8,128)}, f32[256,128]{1,0:T(8,128)}, u32[]{:S(2)}, u32[]{:S(2)}) collective-permute-start(f32[256,128]{1,0:T(8,128)} %get-tuple-element.865), channel_id=1, source_target_pairs={{4,0},{5,1},{6,2},{7,3},{8,4},{9,5},{10,6},{11,7},{12,8},{13,9},{1... | collective-permute-start | bytes 393224 | tf_op jit(solution)/shard_map/ppermute | solution.py:14
  1020.1 102.1 %collective-permute-start.40 = (f32[256,128]{1,0:T(8,128)}, f32[256,128]{1,0:T(8,128)}, u32[]{:S(2)}, u32[]{:S(2)}) collective-permute-start(f32[256,128]{1,0:T(8,128)} %get-tuple-element.866), channel_id=1, source_target_pairs={{5,0},{6,1},{7,2},{8,3},{9,4},{10,5},{11,6},{12,7},{13,8},{14,9},{... | collective-permute-start | bytes 393224 | tf_op jit(solution)/shard_map/ppermute | solution.py:14
  1023.7 105.0 %collective-permute-start.41 = (f32[256,128]{1,0:T(8,128)}, f32[256,128]{1,0:T(8,128)}, u32[]{:S(2)}, u32[]{:S(2)}) collective-permute-start(f32[256,128]{1,0:T(8,128)} %get-tuple-element.867), channel_id=1, source_target_pairs={{6,0},{7,1},{8,2},{9,3},{10,4},{11,5},{12,6},{13,7},{14,8},{15,9},... | collective-permute-start | bytes 393224 | tf_op jit(solution)/shard_map/ppermute | solution.py:14
  1030.8 99.9 %collective-permute-start.42 = (f32[256,128]{1,0:T(8,128)}, f32[256,128]{1,0:T(8,128)}, u32[]{:S(2)}, u32[]{:S(2)}) collective-permute-start(f32[256,128]{1,0:T(8,128)} %get-tuple-element.4043), channel_id=1, source_target_pairs={{7,0},{8,1},{9,2},{10,3},{11,4},{12,5},{13,6},{14,7},{15,8},{16,9}... | collective-permute-start | bytes 393224 | tf_op jit(solution)/shard_map/ppermute | solution.py:14
  1034.6 101.0 %collective-permute-start.43 = (f32[256,128]{1,0:T(8,128)}, f32[256,128]{1,0:T(8,128)}, u32[]{:S(2)}, u32[]{:S(2)}) collective-permute-start(f32[256,128]{1,0:T(8,128)} %get-tuple-element.4023), channel_id=1, source_target_pairs={{8,0},{9,1},{10,2},{11,3},{12,4},{13,5},{14,6},{15,7},{16,8},{17,9... | collective-permute-start | bytes 393224 | tf_op jit(solution)/shard_map/ppermute | solution.py:14
  1041.2 96.7 %collective-permute-start.44 = (f32[256,128]{1,0:T(8,128)}, f32[256,128]{1,0:T(8,128)}, u32[]{:S(2)}, u32[]{:S(2)}) collective-permute-start(f32[256,128]{1,0:T(8,128)} %get-tuple-element.4003), channel_id=1, source_target_pairs={{9,0},{10,1},{11,2},{12,3},{13,4},{14,5},{15,6},{16,7},{17,8},{18,... | collective-permute-start | bytes 393224 | tf_op jit(solution)/shard_map/ppermute | solution.py:14
  1138.0 85.1 %collective-permute-start.25 = (f32[256,128]{1,0:T(8,128)}, f32[256,128]{1,0:T(8,128)}, u32[]{:S(2)}, u32[]{:S(2)}) collective-permute-start(f32[256,128]{1,0:T(8,128)} %copy-done.13), channel_id=1, source_target_pairs={{2,0},{3,1},{4,2},{5,3},{6,4},{7,5},{8,6},{9,7},{10,8},{11,9},{12,... | collective-permute-start | bytes 393224 | tf_op jit(solution)/shard_map/ppermute | solution.py:14
  (585 other events, 1195.1 us)
where the time goes:
time: 1300 us; the launch traced here: 1280 us
  matrix products  508 us (39%)
  loops' own time  274 us (21%)
  local copies, waits for them, and re-layouts  259 us (20%)
  starting transfers between devices  196 us (15%)
  waiting for transfers between devices  21.8 us (2%)
  other arithmetic  18 us (1%)
    another operation x13, loops' own time, pair_grads(): lax.scan(one_head, (zero_rows, zero_keys, zero_keys), jnp.arange(head_cou...  274 us
    ppermute x48, starting transfers between devices, shifted(): return lax.ppermute(block, axis, route)  196 us
    while x1088, local copies, waits for them, and re-layouts  186 us
    dot_general x104, matrix products, one_head(): jnp.dot(dscore, key_states, preferred_element_type=jnp.float32) * inv_root  138 us
    dot_general x104, matrix products, one_head(): dprob = jnp.dot(dout_h, value_states.T, preferred_element_type=jnp.float32)  108 us
    dot_general x104, matrix products, one_head(): jnp.dot(query_h, key_states.T, preferred_element_type=jnp.float32)  105 us
    dot_general x104, matrix products, one_head(): jnp.dot(prob_b.T, dout_h, preferred_element_type=jnp.float32)  95.4 us
    dot_general x104, matrix products, one_head(): jnp.dot(dscore.T, query_h, preferred_element_type=jnp.float32) * inv_root  61.4 us
  transfers between devices with their start and end apart: 48, of which 4 were waited for; matrix products, arithmetic and copies ran while one was open for 46% of the time, Pallas kernels for 0%

commit v1 on v0

v1 whole, which is shorter than its diff:
```python
import math

import jax
import jax.numpy as jnp
from jax import lax
from jax.experimental import pallas as pl
from jax.experimental.pallas import tpu as pltpu
from jax.sharding import PartitionSpec as P

MESH = pl.DeviceIdType.MESH
F32 = jnp.float32
BF16 = jnp.bfloat16
HEADS = 8
DH = 128
TOK = 256
UNITS = 13
SCALE = 1.0 / math.sqrt(DH)
LOG2E = math.log2(math.e)


def dot_nt(a, b):
    return lax.dot_general(a, b, (((1,), (1,)), ((), ())), preferred_element_type=F32)


def dot_nn(a, b):
    return jnp.dot(a, b, preferred_element_type=F32)


def kernel(
    q_hbm, do_hbm, lse_hbm, del_hbm, off_hbm, k_hbm, v_hbm,
    dq_out, dk_out, dv_out,
    q_buf, do_buf, lse_buf, del_buf, off_buf, kv, acc, dqt, dq_in, stage, came_in,
    dq_st, dkv_st,
    load_sem, ex_send, ex_recv, kv_send, kv_recv, g_send, g_recv, dq_sem, out_sem,
):
    outer, inner = lax.axis_size("outer"), lax.axis_size("inner")
    total = outer * inner
    me = lax.axis_index("outer") * inner + lax.axis_index("inner")
    core = lax.rem(me, 2)
    greet = jnp.where(lax.axis_index("inner") < 8, 1, 0)

    def at(chips):
        there = lax.rem(me + 2 * chips + total, total)
        return (lax.div(there, inner), lax.rem(there, inner))

    sib_index = me + 1 - 2 * core
    sibling = (lax.div(sib_index, inner), lax.rem(sib_index, inner))

    loads = [
        pltpu.make_async_copy(src, dst, load_sem.at[n])
        for n, (src, dst) in enumerate((
            (k_hbm, kv.at[0, 0]), (v_hbm, kv.at[0, 1]),
            (q_hbm, q_buf.at[0]), (do_hbm, do_buf.at[0]),
            (lse_hbm, lse_buf.at[0]), (del_hbm, del_buf.at[0]), (off_hbm, off_buf.at[0]),
        ))
    ]
    for load in loads:
        load.start()

    barrier = pltpu.get_barrier_semaphore()
    partners = [sibling] + [at(chips) for chips in (1, -1, 6, -6)]
    for partner in partners:
        pl.semaphore_signal(barrier, inc=1, device_id=partner, device_id_type=MESH)

    def remote(src, dst, send, recv, where):
        return pltpu.make_async_remote_copy(
            src_ref=src, dst_ref=dst, send_sem=send, recv_sem=recv, device_id=where, device_id_type=MESH
        )

    exchange = [
        remote(src, dst, ex_send.at[n], ex_recv.at[n], sibling)
        for n, (src, dst) in enumerate((
            (q_hbm, q_buf.at[1]), (do_hbm, do_buf.at[1]),
            (lse_hbm, lse_buf.at[1]), (del_hbm, del_buf.at[1]), (off_hbm, off_buf.at[1]),
        ))
    ]
    kv_from = {1: (0, 1), 2: (1, 1), 3: (2, 1), 4: (3, 1), 6: (0, 6), 5: (6, -1)}
    kv_copy = {
        j: remote(kv.at[src], kv.at[j], kv_send.at[j], kv_recv.at[j], at(chips))
        for j, (src, chips) in kv_from.items()
    }
    g_to = {j: (came_in.at[j], -1) for j in (3, 2, 1)} | {j: (came_in.at[j], 1) for j in (4, 5)} | {6: (came_in.at[6], -6)}
    g_copy = {
        j: remote(stage.at[j], dst, g_send.at[j], g_recv.at[j], at(chips)) for j, (dst, chips) in g_to.items()
    }
    dq_copy = remote(dqt.at[1], dq_in, dq_sem.at[0], dq_sem.at[1], sibling)

    acc[...] = jnp.zeros_like(acc)
    dqt[...] = jnp.zeros_like(dqt)
    for load in loads:
        load.wait()
    lse_buf[0] = lse_buf[0] * LOG2E

    def arrive(j, *forward):
        kv_copy[j].wait_recv()
        for later in forward:
            kv_copy[later].start()

    def send(j, before=None):
        if before is None:
            stage[j] = acc[j].astype(BF16)
        else:
            g_copy[before].wait_recv()
            stage[j] = (acc[j] + came_in[before].astype(F32)).astype(BF16)
        g_copy[j].start()

    def step(v, carry):
        @pl.when(v == core + greet)
        def _():
            pl.semaphore_wait(barrier, len(partners))
            kv_copy[1].start()
            kv_copy[6].start()
            for copy in exchange:
                copy.start()

        @pl.when(v == core + 1)
        def _():
            for copy in exchange:
                copy.wait_recv()
            lse_buf[1] = lse_buf[1] * LOG2E

        @pl.when(v == 2)
        def _():
            arrive(1, 2)

        @pl.when(v == 4)
        def _():
            arrive(2, 3)
            arrive(6, 5)

        @pl.when(v == 6)
        def _():
            arrive(3, 4)

        @pl.when(v == 8)
        def _():
            send(3)
            arrive(4)

        @pl.when(v == 10)
        def _():
            send(4)
            send(2, 3)
            arrive(5)

        @pl.when(v == 11 + 2 * core)
        def _():
            dq_copy.start()

        @pl.when(v == 12)
        def _():
            send(5, 4)
            send(1, 2)

        j = lax.div(v, 2)
        even = lax.rem(v, 2) == 0
        other = jnp.where(core == 0, (v == 1) | (even & (v > 1) & (v < 12)), even)
        rows = jnp.where(other, 1, 0)
        ahead = TOK * (2 * j + rows * (1 - 2 * core))

        k = kv[j, 0]
        v = kv[j, 1]
        kt = k.T
        local = lax.broadcasted_iota(jnp.int32, (1, TOK), 1)
        high = local + ahead
        low = high - off_buf[rows]
        key_pos = lax.broadcasted_iota(jnp.int32, (TOK, TOK), 0)
        allowed = (key_pos >= low) & (key_pos <= high)
        dk = dv = None
        for h in range(HEADS):
            cols = slice(h * DH, (h + 1) * DH)
            q = q_buf[rows, :, cols]
            do = do_buf[rows, :, cols]
            score = dot_nt(k, q)
            prob = jnp.exp2(score * (SCALE * LOG2E) - lse_buf[rows, h : h + 1, :])
            prob = jnp.where(allowed, prob, 0.0)
            dprob = dot_nt(v, do)
            dscore = (prob * (dprob - del_buf[rows, h : h + 1, :])).astype(BF16)
            dv_h = dot_nn(prob.astype(BF16), do)
            dk_h = dot_nn(dscore, q)
            dv = dv_h if dv is None else dv + dv_h
            dk = dk_h if dk is None else dk + dk_h
            dqt[rows, h] += dot_nn(kt, dscore)
        acc[j, 0] += dk
        acc[j, 1] += dv
        return carry

    lax.fori_loop(core, UNITS + core, step, 0)
    send(6, 5)

    dq_copy.wait_recv()
    for h in range(HEADS):
        dq_st[:, h * DH : (h + 1) * DH] = (((dqt[0, h] + dq_in[h]) * SCALE).T).astype(BF16)
    outs = [pltpu.make_async_copy(dq_st, dq_out, out_sem.at[0])]
    outs[0].start()
    for j in (1, 6):
        g_copy[j].wait_recv()
    for n, (dst, scale) in enumerate(((dk_out, SCALE), (dv_out, 1.0))):
        summed = acc[0, n] + came_in[1, n].astype(F32) + came_in[6, n].astype(F32)
        dkv_st[n] = (summed * scale).astype(BF16)
        copy = pltpu.make_async_copy(dkv_st.at[n], dst, out_sem.at[1 + n])
        copy.start()
        outs.append(copy)
    for copy in exchange:
        copy.wait_send()
    for j in range(1, 7):
        kv_copy[j].wait_send()
        g_copy[j].wait_send()
    dq_copy.wait_send()
    for copy in outs:
        copy.wait()


def on_device(queries, out_grad, logsumexp, row_delta, doc_offset, key_states, value_states):
    kv_block = (2, TOK, DH)
    rows = (TOK, HEADS * DH)
    dma = pltpu.SemaphoreType.DMA
    return pl.pallas_call(
        kernel,
        out_shape=(
            jax.ShapeDtypeStruct(rows, BF16),
            jax.ShapeDtypeStruct((TOK, DH), BF16),
            jax.ShapeDtypeStruct((TOK, DH), BF16),
        ),
        in_specs=[pl.BlockSpec(memory_space=pl.ANY)] * 7,
        out_specs=[pl.BlockSpec(memory_space=pl.ANY)] * 3,
        scratch_shapes=[
            pltpu.VMEM((2, *rows), BF16),
            pltpu.VMEM((2, *rows), BF16),
            pltpu.VMEM((2, HEADS, TOK), F32),
            pltpu.VMEM((2, HEADS, TOK), F32),
            pltpu.VMEM((2, 1, TOK), jnp.int32),
            pltpu.VMEM((7, *kv_block), BF16),
            pltpu.VMEM((7, *kv_block), F32),
            pltpu.VMEM((2, HEADS, DH, TOK), F32),
            pltpu.VMEM((HEADS, DH, TOK), F32),
            pltpu.VMEM((7, *kv_block), BF16),
            pltpu.VMEM((7, *kv_block), BF16),
            pltpu.VMEM(rows, BF16),
            pltpu.VMEM(kv_block, BF16),
            dma((7,)), dma((5,)), dma((5,)), dma((7,)), dma((7,)), dma((7,)), dma((7,)), dma((2,)), dma((3,)),
        ],
        compiler_params=pltpu.CompilerParams(
            collective_id=0, has_side_effects=True, vmem_limit_bytes=60 << 20
        ),
        cost_estimate=pl.CostEstimate(flops=9_000_000_000, bytes_accessed=6_000_000, transcendentals=6_800_000),
        name="packed_attention_backward",
    )(queries, out_grad, logsumexp, row_delta, doc_offset.reshape(1, TOK), key_states, value_states)


def solution(mesh):
    both = ("outer", "inner")
    return jax.shard_map(
        on_device,
        mesh=mesh,
        in_specs=(P(both, None), P(both, None), P(None, both), P(None, both), P(both), P(both, None), P(both, None)),
        out_specs=(P(both, None), P(both, None), P(both, None)),
        check_vma=False,
    )
```

time: 1300 us -> 59 us (0.05)
  the two profiles are of different devices: /device:TPU:37 before, /device:TPU:94 now
where the time goes in v1:
time: 59 us; the launch traced here: 58.8 us
  Pallas kernels  54.8 us (93%)
  local copies, waits for them, and re-layouts  3.4 us (6%)
  between operations  0.65 us (1%)
    pallas_call x1, Pallas kernels, on_device(): pl.pallas_call(kernel, out_shape=(jax.ShapeDtypeStruct(rows, BF16), jax.S...  54.8 us
    unnamed x7, local copies, waits for them, and re-layouts  3.4 us

profile of v1, /device:TPU:94, one launch (start us, length us, event | category | flops | bytes accessed | tf_op | source)
XLA Modules:
  0.0 58.8 jit_solution(18174427734424054922)
XLA Ops:
  0.6 54.8 %packed_attention_backward.1 = (bf16[256,1024]{1,0:T(8,128)(2,1)}, bf16[256,128]{1,0:T(8,128)(2,1)}, bf16[256,128]{1,0:T(8,128)(2,1)}) custom-call(bf16[256,1024]{1,0:T(8,128)(2,1)} %q_hbm.1, bf16[256,1024]{1,0:T(8,128)(2,1)} %do_hbm.1, f32[8,256]{1,0:T(8,128)} %lse_hbm.1, f32[8,256]{1,0:T(8,128)} %del_hbm.1, s32[1,256]{1,0:T(1,128)} %bitcast.1, ...), custom_call_target="tpu_custom_call" | custom-call | flops 8999999488 | bytes 6000000 | tf_op jit(solution)/shard_map/packed_attention_backward/pallas_call | solution.py:218
  55.4 0.0 copy-start.1
  55.4 1.9 %copy.13 = bf16[256,1024]{1,0:T(8,128)(2,1)} copy(bf16[256,1024]{1,0:T(8,128)(2,1)} %get-tuple-element.6) | data formatting | bytes 1048576
  57.3 0.0 copy-done.1
  57.3 0.0 copy-start
  57.3 0.6 %copy.14 = bf16[256,128]{1,0:T(8,128)(2,1)} copy(bf16[256,128]{1,0:T(8,128)(2,1)S(1)} %copy-done.1) | data formatting | bytes 131072
  58.0 0.2 copy-done
  58.2 0.6 %copy.15 = bf16[256,128]{1,0:T(8,128)(2,1)} copy(bf16[256,128]{1,0:T(8,128)(2,1)S(1)} %copy-done) | data formatting | bytes 131072
Async XLA Ops:
  55.4 1.9 %copy-start.1 = (bf16[256,128]{1,0:T(8,128)(2,1)S(1)}, bf16[256,128]{1,0:T(8,128)(2,1)}, u32[]{:S(2)}) copy-start(bf16[256,128]{1,0:T(8,128)(2,1)} %get-tuple-element.7) | copy-start | bytes 196612
  57.3 0.9 %copy-start = (bf16[256,128]{1,0:T(8,128)(2,1)S(1)}, bf16[256,128]{1,0:T(8,128)(2,1)}, u32[]{:S(2)}) copy-start(bf16[256,128]{1,0:T(8,128)(2,1)} %get-tuple-element.8) | copy-start | bytes 196612

commit v2 on v1

--- a/solution.py
+++ b/solution.py
@@ -13,7 +13,6 @@
 HEADS = 8
 DH = 128
 TOK = 256
-UNITS = 13
 SCALE = 1.0 / math.sqrt(DH)
 LOG2E = math.log2(math.e)
 
@@ -37,7 +36,7 @@
     total = outer * inner
     me = lax.axis_index("outer") * inner + lax.axis_index("inner")
     core = lax.rem(me, 2)
-    greet = jnp.where(lax.axis_index("inner") < 8, 1, 0)
+    greet = 0
 
     def at(chips):
         there = lax.rem(me + 2 * chips + total, total)
@@ -58,7 +57,7 @@
         load.start()
 
     barrier = pltpu.get_barrier_semaphore()
-    partners = [sibling] + [at(chips) for chips in (1, -1, 6, -6)]
+    partners = [sibling] + [at(chips) for chips in (1, -1, -6)]
     for partner in partners:
         pl.semaphore_signal(barrier, inc=1, device_id=partner, device_id_type=MESH)
 
@@ -74,14 +73,14 @@
             (lse_hbm, lse_buf.at[1]), (del_hbm, del_buf.at[1]), (off_hbm, off_buf.at[1]),
         ))
     ]
-    kv_from = {1: (0, 1), 2: (1, 1), 3: (2, 1), 4: (3, 1), 6: (0, 6), 5: (6, -1)}
+    kv_from = {1: (0, 1), 2: (1, 1), 3: (2, 1), 6: (0, 6), 5: (6, -1), 4: (5, -1)}
     kv_copy = {
         j: remote(kv.at[src], kv.at[j], kv_send.at[j], kv_recv.at[j], at(chips))
         for j, (src, chips) in kv_from.items()
     }
-    g_to = {j: (came_in.at[j], -1) for j in (3, 2, 1)} | {j: (came_in.at[j], 1) for j in (4, 5)} | {6: (came_in.at[6], -6)}
+    g_to = {1: -1, 2: -1, 3: -1, 4: -1, 5: -1, 6: -1}
     g_copy = {
-        j: remote(stage.at[j], dst, g_send.at[j], g_recv.at[j], at(chips)) for j, (dst, chips) in g_to.items()
+        j: remote(stage.at[j], came_in.at[j], g_send.at[j], g_recv.at[j], at(chips)) for j, chips in g_to.items()
     }
     dq_copy = remote(dqt.at[1], dq_in, dq_sem.at[0], dq_sem.at[1], sibling)
 
@@ -104,8 +103,36 @@
             stage[j] = (acc[j] + came_in[before].astype(F32)).astype(BF16)
         g_copy[j].start()
 
-    def step(v, carry):
-        @pl.when(v == core + greet)
+    def tiles(j, row_blocks):
+        k = kv[j, 0]
+        v = kv[j, 1]
+        kt = k.T
+        local = lax.broadcasted_iota(jnp.int32, (1, TOK), 1)
+        key_pos = lax.broadcasted_iota(jnp.int32, (TOK, TOK), 0)
+        dk = dv = None
+        for rows in row_blocks:
+            high = local + TOK * (2 * j + rows * (1 - 2 * core))
+            low = high - off_buf[rows]
+            allowed = (key_pos >= low) & (key_pos <= high)
+            for h in range(HEADS):
+                cols = slice(h * DH, (h + 1) * DH)
+                q = q_buf[rows, :, cols]
+                do = do_buf[rows, :, cols]
+                score = dot_nt(k, q)
+                prob = jnp.exp2(score * (SCALE * LOG2E) - lse_buf[rows, h : h + 1, :])
+                prob = jnp.where(allowed, prob, 0.0)
+                dprob = dot_nt(v, do)
+                dscore = (prob * (dprob - del_buf[rows, h : h + 1, :])).astype(BF16)
+                dv_h = dot_nn(prob.astype(BF16), do)
+                dk_h = dot_nn(dscore, q)
+                dv = dv_h if dv is None else dv + dv_h
+                dk = dk_h if dk is None else dk + dk_h
+                dqt[rows, h] += dot_nn(kt, dscore)
+        acc[j, 0] += dk
+        acc[j, 1] += dv
+
+    def single(u, carry):
+        @pl.when(u == greet)
         def _():
             pl.semaphore_wait(barrier, len(partners))
             kv_copy[1].start()
@@ -113,90 +140,67 @@
             for copy in exchange:
                 copy.start()
 
-        @pl.when(v == core + 1)
+        @pl.when(u == 1)
         def _():
             for copy in exchange:
                 copy.wait_recv()
             lse_buf[1] = lse_buf[1] * LOG2E
 
-        @pl.when(v == 2)
+        @pl.when(u == 2 - core)
+        def _():
+            arrive(6, 5)
+
+        @pl.when(u == 2)
         def _():
             arrive(1, 2)
 
-        @pl.when(v == 4)
-        def _():
+        tiles(6 * lax.div(u + core, 2), (lax.rem(u, 2),))
+        return carry
+
+    def double(t, carry):
+        @pl.when(t == 0)
+        def _():
+            arrive(5, 4)
+            send(6)
             arrive(2, 3)
-            arrive(6, 5)
-
-        @pl.when(v == 6)
-        def _():
-            arrive(3, 4)
-
-        @pl.when(v == 8)
-        def _():
-            send(3)
+
+        @pl.when(t == 1)
+        def _():
             arrive(4)
-
-        @pl.when(v == 10)
-        def _():
-            send(4)
+            send(5, 6)
+
+        @pl.when(t == 2)
+        def _():
+            arrive(3)
+            send(4, 5)
+
+        @pl.when(t == 3)
+        def _():
+            send(3, 4)
+
+        @pl.when(t == 4)
+        def _():
             send(2, 3)
-            arrive(5)
-
-        @pl.when(v == 11 + 2 * core)
-        def _():
-            dq_copy.start()
-
-        @pl.when(v == 12)
-        def _():
-            send(5, 4)
-            send(1, 2)
-
-        j = lax.div(v, 2)
-        even = lax.rem(v, 2) == 0
-        other = jnp.where(core == 0, (v == 1) | (even & (v > 1) & (v < 12)), even)
-        rows = jnp.where(other, 1, 0)
-        ahead = TOK * (2 * j + rows * (1 - 2 * core))
-
-        k = kv[j, 0]
-        v = kv[j, 1]
-        kt = k.T
-        local = lax.broadcasted_iota(jnp.int32, (1, TOK), 1)
-        high = local + ahead
-        low = high - off_buf[rows]
-        key_pos = lax.broadcasted_iota(jnp.int32, (TOK, TOK), 0)
-        allowed = (key_pos >= low) & (key_pos <= high)
-        dk = dv = None
-        for h in range(HEADS):
-            cols = slice(h * DH, (h + 1) * DH)
-            q = q_buf[rows, :, cols]
-            do = do_buf[rows, :, cols]
-            score = dot_nt(k, q)
-            prob = jnp.exp2(score * (SCALE * LOG2E) - lse_buf[rows, h : h + 1, :])
-            prob = jnp.where(allowed, prob, 0.0)
-            dprob = dot_nt(v, do)
-            dscore = (prob * (dprob - del_buf[rows, h : h + 1, :])).astype(BF16)
-            dv_h = dot_nn(prob.astype(BF16), do)
-            dk_h = dot_nn(dscore, q)
-            dv = dv_h if dv is None else dv + dv_h
-            dk = dk_h if dk is None else dk + dk_h
-            dqt[rows, h] += dot_nn(kt, dscore)
-        acc[j, 0] += dk
-        acc[j, 1] += dv
+
+        tiles(5 - t, (1, 0))
         return carry
 
-    lax.fori_loop(core, UNITS + core, step, 0)
-    send(6, 5)
+    lax.fori_loop(0, 3, single, 0)
+    lax.fori_loop(0, 5, double, 0)
+    dq_copy.start()
+    send(1, 2)
 
     dq_copy.wait_recv()
     for h in range(HEADS):
         dq_st[:, h * DH : (h + 1) * DH] = (((dqt[0, h] + dq_in[h]) * SCALE).T).astype(BF16)
     outs = [pltpu.make_async_copy(dq_st, dq_out, out_sem.at[0])]
     outs[0].start()
-    for j in (1, 6):
+    for j in (1,):
         g_copy[j].wait_recv()
     for n, (dst, scale) in enumerate(((dk_out, SCALE), (dv_out, 1.0))):
-        summed = acc[0, n] + came_in[1, n].astype(F32) + came_in[6, n].astype(F32)
+        summed = acc[0, n]
+        for j in (1,):
+            summed = summed + came_in[j, n].astype(F32)
         dkv_st[n] = (summed * scale).astype(BF16)
         copy = pltpu.make_async_copy(dkv_st.at[n], dst, out_sem.at[1 + n])
         copy.start()
@@ -211,17 +215,24 @@
         copy.wait()
 
 
+def place(dq_in, dk_in, dv_in, dq_out, dk_out, dv_out):
+    dq_out[...] = dq_in[...]
+    dk_out[...] = dk_in[...]
+    dv_out[...] = dv_in[...]
+
+
 def on_device(queries, out_grad, logsumexp, row_delta, doc_offset, key_states, value_states):
     kv_block = (2, TOK, DH)
     rows = (TOK, HEADS * DH)
     dma = pltpu.SemaphoreType.DMA
-    return pl.pallas_call(
+    shapes = (
+        jax.ShapeDtypeStruct(rows, BF16),
+        jax.ShapeDtypeStruct((TOK, DH), BF16),
+        jax.ShapeDtypeStruct((TOK, DH), BF16),
+    )
+    grads = pl.pallas_call(
         kernel,
-        out_shape=(
-            jax.ShapeDtypeStruct(rows, BF16),
-            jax.ShapeDtypeStruct((TOK, DH), BF16),
-            jax.ShapeDtypeStruct((TOK, DH), BF16),
-        ),
+        out_shape=shapes,
         in_specs=[pl.BlockSpec(memory_space=pl.ANY)] * 7,
         out_specs=[pl.BlockSpec(memory_space=pl.ANY)] * 3,
         scratch_shapes=[
@@ -246,6 +257,7 @@
         cost_estimate=pl.CostEstimate(flops=9_000_000_000, bytes_accessed=6_000_000, transcendentals=6_800_000),
         name="packed_attention_backward",
     )(queries, out_grad, logsumexp, row_delta, doc_offset.reshape(1, TOK), key_states, value_states)
+    return pl.pallas_call(place, out_shape=shapes, name="place")(*grads)
 
 
 def solution(mesh):

time: 59 us -> 54.8 us (0.929)
  the two profiles are of different devices: /device:TPU:94 before, /device:TPU:1 now
where the time goes in v2:
time: 54.8 us; the launch traced here: 54.7 us
  Pallas kernels  54.1 us (99%)
  between operations  0.64 us (1%)
    pallas_call x1, Pallas kernels, on_device(): pl.pallas_call(kernel, out_shape=shapes, in_specs=[pl.BlockSpec(memory_sp...  52.1 us
    pallas_call x1, Pallas kernels, on_device(): return pl.pallas_call(place, out_shape=shapes, name='place')(*grads)  1.92 us

profile of v2, /device:TPU:1, one launch (start us, length us, event | category | flops | bytes accessed | tf_op | source)
XLA Modules:
  0.0 54.7 jit_solution(7136863537345801009)
XLA Ops:
  0.6 52.1 %packed_attention_backward.1 = (bf16[256,1024]{1,0:T(8,128)(2,1)}, bf16[256,128]{1,0:T(8,128)(2,1)}, bf16[256,128]{1,0:T(8,128)(2,1)}) custom-call(bf16[256,1024]{1,0:T(8,128)(2,1)} %q_hbm.1, bf16[256,1024]{1,0:T(8,128)(2,1)} %do_hbm.1, f32[8,256]{1,0:T(8,128)} %lse_hbm.1, f32[8,256]{1,0:T(8,128)} %del_hbm.1, s32[1,256]{1,0:T(1,128)} %bitcast.1, ...), custom_call_target="tpu_custom_call" | custom-call | flops 8999999488 | bytes 6000000 | tf_op jit(solution)/shard_map/packed_attention_backward/pallas_call | solution.py:233
  52.8 1.9 %place.1 = (bf16[256,1024]{1,0:T(8,128)(2,1)}, bf16[256,128]{1,0:T(8,128)(2,1)}, bf16[256,128]{1,0:T(8,128)(2,1)}) custom-call(bf16[256,1024]{1,0:T(8,128)(2,1)} %get-tuple-element.6.dq_in, bf16[256,128]{1,0:T(8,128)(2,1)} %get-tuple-element.7.dk_in, bf16[256,128]{1,0:T(8,128)(2,1)} %get-tuple-element.8.dv_in), custom_call_target="tpu_custom_call" | custom-call | tf_op jit(solution)/shard_map/place/pallas_call | solution.py:260

commit v3 on v2

--- a/solution.py
+++ b/solution.py
@@ -29,8 +29,9 @@
     q_hbm, do_hbm, lse_hbm, del_hbm, off_hbm, k_hbm, v_hbm,
     dq_out, dk_out, dv_out,
     q_buf, do_buf, lse_buf, del_buf, off_buf, kv, acc, dqt, dq_in, stage, came_in,
-    dq_st, dkv_st,
+    dq_st, dkv_st, spare,
     load_sem, ex_send, ex_recv, kv_send, kv_recv, g_send, g_recv, dq_sem, out_sem,
+    help_send, help_recv,
 ):
     outer, inner = lax.axis_size("outer"), lax.axis_size("inner")
     total = outer * inner
@@ -57,9 +58,18 @@
         load.start()
 
     barrier = pltpu.get_barrier_semaphore()
-    partners = [sibling] + [at(chips) for chips in (1, -1, -6)]
-    for partner in partners:
-        pl.semaphore_signal(barrier, inc=1, device_id=partner, device_id_type=MESH)
+    chip, last = lax.div(me, 2), total // 2 - 1
+    before = chip >= 1
+    after = chip < last
+    sixth = chip + 6 <= last
+    short = (chip == last - 5) | (chip == last - 4)
+    helper = (chip == last - 7) | (chip == last - 6)
+    pl.semaphore_signal(barrier, inc=1, device_id=sibling, device_id_type=MESH)
+    told = ((after, 1), (before, -1), (chip >= 6, -6), (helper, 2), (chip == last, -7))
+    for there, chips in told:
+        @pl.when(there)
+        def _():
+            pl.semaphore_signal(barrier, inc=1, device_id=at(chips), device_id_type=MESH)
 
     def remote(src, dst, send, recv, where):
         return pltpu.make_async_remote_copy(
@@ -78,6 +88,12 @@
         j: remote(kv.at[src], kv.at[j], kv_send.at[j], kv_recv.at[j], at(chips))
         for j, (src, chips) in kv_from.items()
     }
+    help_copy = [
+        remote(kv.at[0], spare.at[0], help_send.at[0], help_recv.at[0], at(-2)),
+        remote(spare.at[0], kv.at[5], help_send.at[1], kv_recv.at[5], at(7)),
+        remote(spare.at[0], spare.at[1], help_send.at[2], help_recv.at[1], at(-1)),
+        remote(spare.at[1], kv.at[4], help_send.at[3], kv_recv.at[4], at(7)),
+    ]
     g_to = {1: -1, 2: -1, 3: -1, 4: -1, 5: -1, 6: -1}
     g_copy = {
         j: remote(stage.at[j], came_in.at[j], g_send.at[j], g_recv.at[j], at(chips)) for j, chips in g_to.items()
@@ -90,18 +106,24 @@
         load.wait()
     lse_buf[0] = lse_buf[0] * LOG2E
 
-    def arrive(j, *forward):
-        kv_copy[j].wait_recv()
-        for later in forward:
-            kv_copy[later].start()
-
-    def send(j, before=None):
-        if before is None:
+    def passes(j):
+        return {1: after, 6: sixth, 2: before & after, 3: (chip >= 2) & after, 5: chip >= 6, 4: chip >= 5}[j]
+
+    def arrive(j, forward=None):
+        pl.when(chip >= j)(kv_copy[j].wait_recv)
+        if forward is not None:
+            pl.when(passes(forward))(kv_copy[forward].start)
+
+    def send(j, chained=None):
+        @pl.when(chip >= j)
+        def _():
             stage[j] = acc[j].astype(BF16)
-        else:
-            g_copy[before].wait_recv()
-            stage[j] = (acc[j] + came_in[before].astype(F32)).astype(BF16)
-        g_copy[j].start()
+            if chained is not None:
+                @pl.when(after)
+                def _():
+                    g_copy[chained].wait_recv()
+                    stage[j] = (acc[j] + came_in[chained].astype(F32)).astype(BF16)
+            g_copy[j].start()
 
     def tiles(j, row_blocks):
         k = kv[j, 0]
@@ -134,9 +156,11 @@
     def single(u, carry):
         @pl.when(u == greet)
         def _():
-            pl.semaphore_wait(barrier, len(partners))
-            kv_copy[1].start()
-            kv_copy[6].start()
+            ready = [jnp.where(there, 1, 0) for there in (after, before, sixth, short, chip == last - 7)]
+            pl.semaphore_wait(barrier, 1 + sum(ready))
+            pl.when(sixth)(kv_copy[6].start)
+            pl.when(after)(kv_copy[1].start)
+            pl.when(short)(help_copy[0].start)
             for copy in exchange:
                 copy.start()
 
@@ -149,12 +173,16 @@
         @pl.when(u == 2 - core)
         def _():
             arrive(6, 5)
+            pl.when(helper)(help_copy[0].wait_recv)
+            pl.when(chip == last - 7)(help_copy[1].start)
+            pl.when(chip == last - 6)(help_copy[2].start)
 
         @pl.when(u == 2)
         def _():
             arrive(1, 2)
 
-        tiles(6 * lax.div(u + core, 2), (lax.rem(u, 2),))
+        j = 6 * lax.div(u + core, 2)
+        pl.when(chip >= j)(lambda: tiles(j, (lax.rem(u, 2),)))
         return carry
 
     def double(t, carry):
@@ -164,6 +192,11 @@
             send(6)
             arrive(2, 3)
 
+            @pl.when(chip == last - 7)
+            def _():
+                help_copy[2].wait_recv()
+                help_copy[3].start()
+
         @pl.when(t == 1)
         def _():
             arrive(4)
@@ -182,7 +215,7 @@
         def _():
             send(2, 3)
 
-        tiles(5 - t, (1, 0))
+        pl.when(chip >= 5 - t)(lambda: tiles(5 - t, (1, 0)))
         return carry
 
     lax.fori_loop(0, 3, single, 0)
@@ -195,21 +228,26 @@
         dq_st[:, h * DH : (h + 1) * DH] = (((dqt[0, h] + dq_in[h]) * SCALE).T).astype(BF16)
     outs = [pltpu.make_async_copy(dq_st, dq_out, out_sem.at[0])]
     outs[0].start()
-    for j in (1,):
-        g_copy[j].wait_recv()
+
+    @pl.when(after)
+    def _():
+        g_copy[1].wait_recv()
+        acc[0] = acc[0] + came_in[1].astype(F32)
+
     for n, (dst, scale) in enumerate(((dk_out, SCALE), (dv_out, 1.0))):
-        summed = acc[0, n]
-        for j in (1,):
-            summed = summed + came_in[j, n].astype(F32)
-        dkv_st[n] = (summed * scale).astype(BF16)
+        dkv_st[n] = (acc[0, n] * scale).astype(BF16)
         copy = pltpu.make_async_copy(dkv_st.at[n], dst, out_sem.at[1 + n])
         copy.start()
         outs.append(copy)
     for copy in exchange:
         copy.wait_send()
     for j in range(1, 7):
-        kv_copy[j].wait_send()
-        g_copy[j].wait_send()
+        pl.when(passes(j))(kv_copy[j].wait_send)
+        pl.when(chip >= j)(g_copy[j].wait_send)
+    pl.when(short)(help_copy[0].wait_send)
+    pl.when(chip == last - 7)(help_copy[1].wait_send)
+    pl.when(chip == last - 6)(help_copy[2].wait_send)
+    pl.when(chip == last - 7)(help_copy[3].wait_send)
     dq_copy.wait_send()
     for copy in outs:
         copy.wait()
@@ -249,7 +287,9 @@
             pltpu.VMEM((7, *kv_block), BF16),
             pltpu.VMEM(rows, BF16),
             pltpu.VMEM(kv_block, BF16),
+            pltpu.VMEM((2, *kv_block), BF16),
             dma((7,)), dma((5,)), dma((5,)), dma((7,)), dma((7,)), dma((7,)), dma((7,)), dma((2,)), dma((3,)),
+            dma((4,)), dma((2,)),
         ],
         compiler_params=pltpu.CompilerParams(
             collective_id=0, has_side_effects=True, vmem_limit_bytes=60 << 20

time: 54.8 us -> 54.3 us (level)
  the two profiles are of different devices: /device:TPU:1 before, /device:TPU:94 now
where the time goes in v3:
time: 54.3 us; the launch traced here: 54.2 us
  Pallas kernels  53.5 us (99%)
  between operations  0.64 us (1%)
    pallas_call x1, Pallas kernels, on_device(): pl.pallas_call(kernel, out_shape=shapes, in_specs=[pl.BlockSpec(memory_sp...  51.6 us
    pallas_call x1, Pallas kernels, on_device(): return pl.pallas_call(place, out_shape=shapes, name='place')(*grads)  1.92 us

profile of v3, /device:TPU:94, one launch (start us, length us, event | category | flops | bytes accessed | tf_op | source)
XLA Modules:
  0.0 54.2 jit_solution(12676761991742562223)
XLA Ops:
  0.6 51.6 %packed_attention_backward.1 = (bf16[256,1024]{1,0:T(8,128)(2,1)}, bf16[256,128]{1,0:T(8,128)(2,1)}, bf16[256,128]{1,0:T(8,128)(2,1)}) custom-call(bf16[256,1024]{1,0:T(8,128)(2,1)} %q_hbm.1, bf16[256,1024]{1,0:T(8,128)(2,1)} %do_hbm.1, f32[8,256]{1,0:T(8,128)} %lse_hbm.1, f32[8,256]{1,0:T(8,128)} %del_hbm.1, s32[1,256]{1,0:T(1,128)} %bitcast.1, ...), custom_call_target="tpu_custom_call" | custom-call | flops 8999999488 | bytes 6000000 | tf_op jit(solution)/shard_map/packed_attention_backward/pallas_call | solution.py:271
  52.2 1.9 %place.1 = (bf16[256,1024]{1,0:T(8,128)(2,1)}, bf16[256,128]{1,0:T(8,128)(2,1)}, bf16[256,128]{1,0:T(8,128)(2,1)}) custom-call(bf16[256,1024]{1,0:T(8,128)(2,1)} %get-tuple-element.6.dq_in, bf16[256,128]{1,0:T(8,128)(2,1)} %get-tuple-element.7.dk_in, bf16[256,128]{1,0:T(8,128)(2,1)} %get-tuple-element.8.dv_in), custom_call_target="tpu_custom_call" | custom-call | tf_op jit(solution)/shard_map/place/pallas_call | solution.py:300

commit v4 on v3

--- a/solution.py
+++ b/solution.py
@@ -23,6 +23,23 @@
 
 def dot_nn(a, b):
     return jnp.dot(a, b, preferred_element_type=F32)
+
+
+class Both:
+    def __init__(self, copies):
+        self.copies = copies
+
+    def start(self):
+        for copy in self.copies:
+            copy.start()
+
+    def wait_recv(self):
+        for copy in self.copies:
+            copy.wait_recv()
+
+    def wait_send(self):
+        for copy in self.copies:
+            copy.wait_send()
 
 
 def kernel(
@@ -76,6 +93,9 @@
             src_ref=src, dst_ref=dst, send_sem=send, recv_sem=recv, device_id=where, device_id_type=MESH
         )
 
+    def halves(src, dst, send, recv, where):
+        return Both([remote(src.at[n], dst.at[n], send.at[n], recv.at[n], where) for n in range(2)])
+
     exchange = [
         remote(src, dst, ex_send.at[n], ex_recv.at[n], sibling)
         for n, (src, dst) in enumerate((
@@ -85,18 +105,18 @@
     ]
     kv_from = {1: (0, 1), 2: (1, 1), 3: (2, 1), 6: (0, 6), 5: (6, -1), 4: (5, -1)}
     kv_copy = {
-        j: remote(kv.at[src], kv.at[j], kv_send.at[j], kv_recv.at[j], at(chips))
+        j: halves(kv.at[src], kv.at[j], kv_send.at[j], kv_recv.at[j], at(chips))
         for j, (src, chips) in kv_from.items()
     }
     help_copy = [
-        remote(kv.at[0], spare.at[0], help_send.at[0], help_recv.at[0], at(-2)),
-        remote(spare.at[0], kv.at[5], help_send.at[1], kv_recv.at[5], at(7)),
-        remote(spare.at[0], spare.at[1], help_send.at[2], help_recv.at[1], at(-1)),
-        remote(spare.at[1], kv.at[4], help_send.at[3], kv_recv.at[4], at(7)),
+        halves(kv.at[0], spare.at[0], help_send.at[0], help_recv.at[0], at(-2)),
+        halves(spare.at[0], kv.at[5], help_send.at[1], kv_recv.at[5], at(7)),
+        halves(spare.at[0], spare.at[1], help_send.at[2], help_recv.at[1], at(-1)),
+        halves(spare.at[1], kv.at[4], help_send.at[3], kv_recv.at[4], at(7)),
     ]
     g_to = {1: -1, 2: -1, 3: -1, 4: -1, 5: -1, 6: -1}
     g_copy = {
-        j: remote(stage.at[j], came_in.at[j], g_send.at[j], g_recv.at[j], at(chips)) for j, chips in g_to.items()
+        j: halves(stage.at[j], came_in.at[j], g_send.at[j], g_recv.at[j], at(chips)) for j, chips in g_to.items()
     }
     dq_copy = remote(dqt.at[1], dq_in, dq_sem.at[0], dq_sem.at[1], sibling)
 
@@ -110,20 +130,23 @@
         return {1: after, 6: sixth, 2: before & after, 3: (chip >= 2) & after, 5: chip >= 6, 4: chip >= 5}[j]
 
     def arrive(j, forward=None):
-        pl.when(chip >= j)(kv_copy[j].wait_recv)
-        if forward is not None:
-            pl.when(passes(forward))(kv_copy[forward].start)
+        for n in range(2):
+            pl.when(chip >= j)(kv_copy[j].copies[n].wait_recv)
+            if forward is not None:
+                pl.when(passes(forward))(kv_copy[forward].copies[n].start)
 
     def send(j, chained=None):
         @pl.when(chip >= j)
         def _():
-            stage[j] = acc[j].astype(BF16)
-            if chained is not None:
-                @pl.when(after)
-                def _():
-                    g_copy[chained].wait_recv()
-                    stage[j] = (acc[j] + came_in[chained].astype(F32)).astype(BF16)
-            g_copy[j].start()
+            for n in range(2):
+                if chained is not None:
+                    @pl.when(after)
+                    def _():
+                        g_copy[chained].copies[n].wait_recv()
+                        acc[j, n] = acc[j, n] + came_in[chained, n].astype(F32)
+
+                stage[j, n] = acc[j, n].astype(BF16)
+                g_copy[j].copies[n].start()
 
     def tiles(j, row_blocks):
         k = kv[j, 0]
@@ -229,12 +252,12 @@
     outs = [pltpu.make_async_copy(dq_st, dq_out, out_sem.at[0])]
     outs[0].start()
 
-    @pl.when(after)
-    def _():
-        g_copy[1].wait_recv()
-        acc[0] = acc[0] + came_in[1].astype(F32)
-
     for n, (dst, scale) in enumerate(((dk_out, SCALE), (dv_out, 1.0))):
+        @pl.when(after)
+        def _():
+            g_copy[1].copies[n].wait_recv()
+            acc[0, n] = acc[0, n] + came_in[1, n].astype(F32)
+
         dkv_st[n] = (acc[0, n] * scale).astype(BF16)
         copy = pltpu.make_async_copy(dkv_st.at[n], dst, out_sem.at[1 + n])
         copy.start()
@@ -288,8 +311,8 @@
             pltpu.VMEM(rows, BF16),
             pltpu.VMEM(kv_block, BF16),
             pltpu.VMEM((2, *kv_block), BF16),
-            dma((7,)), dma((5,)), dma((5,)), dma((7,)), dma((7,)), dma((7,)), dma((7,)), dma((2,)), dma((3,)),
-            dma((4,)), dma((2,)),
+            dma((7,)), dma((5,)), dma((5,)), dma((7, 2)), dma((7, 2)), dma((7, 2)), dma((7, 2)), dma((2,)), dma((3,)),
+            dma((4, 2)), dma((2, 2)),
         ],
         compiler_params=pltpu.CompilerParams(
             collective_id=0, has_side_effects=True, vmem_limit_bytes=60 << 20

time: 54.3 us -> 52.8 us (0.972)
  the two profiles are of different devices: /device:TPU:94 before, /device:TPU:4 now
where the time goes in v4:
time: 52.8 us; the launch traced here: 52.7 us
  Pallas kernels  52.1 us (99%)
  between operations  0.64 us (1%)
    pallas_call x1, Pallas kernels, on_device(): pl.pallas_call(kernel, out_shape=shapes, in_specs=[pl.BlockSpec(memory_sp...  50.1 us
    pallas_call x1, Pallas kernels, on_device(): return pl.pallas_call(place, out_shape=shapes, name='place')(*grads)  1.92 us

profile of v4, /device:TPU:4, one launch (start us, length us, event | category | flops | bytes accessed | tf_op | source)
XLA Modules:
  0.0 52.7 jit_solution(8836307111360505125)
XLA Ops:
  0.6 50.1 %packed_attention_backward.1 = (bf16[256,1024]{1,0:T(8,128)(2,1)}, bf16[256,128]{1,0:T(8,128)(2,1)}, bf16[256,128]{1,0:T(8,128)(2,1)}) custom-call(bf16[256,1024]{1,0:T(8,128)(2,1)} %q_hbm.1, bf16[256,1024]{1,0:T(8,128)(2,1)} %do_hbm.1, f32[8,256]{1,0:T(8,128)} %lse_hbm.1, f32[8,256]{1,0:T(8,128)} %del_hbm.1, s32[1,256]{1,0:T(1,128)} %bitcast.1, ...), custom_call_target="tpu_custom_call" | custom-call | flops 8999999488 | bytes 6000000 | tf_op jit(solution)/shard_map/packed_attention_backward/pallas_call | solution.py:294
  50.8 1.9 %place.1 = (bf16[256,1024]{1,0:T(8,128)(2,1)}, bf16[256,128]{1,0:T(8,128)(2,1)}, bf16[256,128]{1,0:T(8,128)(2,1)}) custom-call(bf16[256,1024]{1,0:T(8,128)(2,1)} %get-tuple-element.6.dq_in, bf16[256,128]{1,0:T(8,128)(2,1)} %get-tuple-element.7.dk_in, bf16[256,128]{1,0:T(8,128)(2,1)} %get-tuple-element.8.dv_in), custom_call_target="tpu_custom_call" | custom-call | tf_op jit(solution)/shard_map/place/pallas_call | solution.py:323
